TPU v7x, 256 devices: a whole 4x4x8 slice. The times are simulated.
256 devices in a mesh: group: 8 (over x_hi, y), fsdp: 32 (over z, x_lo, core).
Axes of the slice: x: 4 (x_hi: 2, x_lo: 2; x = x_hi * 2 + x_lo), y: 4, z: 8, core: 2. Of those that a mesh axis runs over, the one named last changes fastest.
Arguments:
- tokens: bfloat16 [131072, 8192], P(('group', 'fsdp')), may hold values from -6 to 6
- target: bfloat16 [131072, 512], P(('group', 'fsdp')), may hold values from -6 to 6
- weight: bfloat16 [8192, 512], P('fsdp'), may hold values from -6 to 6
- momentum: float32 [8192, 512], P('fsdp', 'group'), may hold values from -4 to 4
Outputs:
- new_weight: bfloat16 [8192, 512], P('fsdp')
- new_momentum: float32 [8192, 512], P('fsdp', 'group')
All inputs are finite; a program needn't handle non-finite values.
Results may differ from a plain program's by a relative error of at most 0.0055.
Values may be sent and summed in bfloat16 or wider, within the bound.
A program may use at most 128 MiB of HBM per device.

v0:
```python
import math

import jax
import jax.numpy as jnp
from jax import lax
from jax.sharding import PartitionSpec as P

BLOCK = 32


inner_rate = 0.5
momentum_decay = 0.9
outer_rate = 0.7


def encode(delta):
    row_count, width_all = delta.shape
    blocked = delta.reshape(row_count, width_all // BLOCK, BLOCK)
    largest = jnp.max(jnp.abs(blocked), axis=2)
    block_scale = jnp.exp2(jnp.ceil(jnp.log2(largest / 6.0 + 1e-30))).astype(jnp.bfloat16)
    scale_wide = block_scale.astype(jnp.float32)[:, :, None]
    code_vals = jnp.clip(blocked / scale_wide, -6.0, 6.0).astype(jnp.bfloat16)
    return (code_vals, block_scale)


def body(tokens, target, weight, momentum):
    tok_count, features = tokens.shape
    shard_rows, out_width = weight.shape
    group_size = lax.axis_size("group")
    group_tokens = tok_count * lax.axis_size("fsdp")
    root_width = math.sqrt(features)
    grad_scale = math.sqrt(features / group_tokens)
    columns = tokens
    values = (
        jnp.dot(
            columns,
            lax.all_gather(weight, "fsdp", axis=0, tiled=True),
            preferred_element_type=jnp.float32,
        )
        / root_width
    )
    cotangent = ((values - target.astype(jnp.float32)) * grad_scale).astype(jnp.bfloat16)
    columns = tokens
    gradient = (
        lax.psum_scatter(
            lax.dot_general(
                columns, cotangent, (((0,), (0,)), ((), ())), preferred_element_type=jnp.float32
            ),
            "fsdp",
            scatter_dimension=0,
            tiled=True,
        )
        / root_width
    )
    code_vals, block_scale = encode(inner_rate * gradient)
    own_width = out_width // group_size
    code_vals, block_scale = lax.optimization_barrier((code_vals, block_scale))
    decoded = code_vals.astype(jnp.float32) * block_scale.astype(jnp.float32)[:, :, None]
    summed = lax.psum_scatter(
        decoded.reshape(shard_rows, out_width), "group", scatter_dimension=1, tiled=True
    )
    average = summed / group_size
    new_momentum = momentum_decay * momentum + average
    own_weight = lax.dynamic_slice_in_dim(weight, lax.axis_index("group") * own_width, own_width, 1)
    updated = (
        own_weight.astype(jnp.float32) - outer_rate * (average + momentum_decay * new_momentum)
    ).astype(jnp.bfloat16)
    new_weight = lax.all_gather(updated, "group", axis=1, tiled=True)
    return (new_weight, new_momentum)


def solution(mesh):
    placed = (
        P(("group", "fsdp"), None),
        P(("group", "fsdp"), None),
        P("fsdp", None),
        P("fsdp", "group"),
    )
    return jax.shard_map(
        body,
        mesh=mesh,
        in_specs=placed,
        out_specs=(P("fsdp", None), P("fsdp", "group")),
        check_vma=False,
    )
```

profile of v0, /device:TPU:2, one launch (start us, length us, event | category | flops | bytes accessed | tf_op | source)
XLA Modules:
  0.0 419.7 jit_solution(1011841525230093356)
XLA Ops:
  7.2 0.0 all-gather.2.cloned.1.call-start
  7.2 0.7 all-gather.2.cloned.1.call-update
  7.9 0.0 reduce-scatter.3.cloned.1.call-start
  7.9 77.2 %all-gather.2.cloned.1.call-done = bf16[8192,512]{1,0:T(8,128)(2,1)} async-done(((bf16[256,512]{1,0:T(8,128)(2,1)}), bf16[8192,512]{1,0:T(8,128)(2,1)}) %all-gather.2.cloned.1.call-update) | async-done | bytes 8388624 | tf_op jit(solution)/shard_map/all_gather | solution.py:37
  85.1 23.0 %convolution_bitcast_fusion = f32[8192,512]{0,1:T(8,128)} fusion(bf16[512,8192]{1,0:T(8,128)(2,1)} %param.4, bf16[8192,512]{1,0:T(8,128)(2,1)} %all-gather.2.cloned.1.call-done, bf16[512,512]{1,0:T(8,128)(2,1)} %param.5), kind=kOutput, calls=%fused_computation | convolution fusion | flops 8591245312 | bytes 34078720 | tf_op jit(solution)/shard_map/dot_general | solution.py:46
  108.1 0.0 copy-start
  108.1 0.0 reduce-scatter.3.cloned.1.call-update
  108.2 0.0 reduce-scatter.5.cloned.1.call-start
  108.2 188.0 %reduce-scatter.3.cloned.1.call-done = f32[256,512]{0,1:T(8,128)} async-done(((f32[8192,512]{0,1:T(8,128)}), f32[256,512]{0,1:T(8,128)}) %reduce-scatter.3.cloned.1.call-update) | async-done | bytes 524304 | tf_op jit(solution)/shard_map/reduce_scatter | solution.py:45
  296.2 1.1 abs_reduce_fusion
  297.4 1.1 clamp_convert_fusion
  298.5 0.8 convert_multiply_fusion
  299.4 0.0 reduce-scatter.5.cloned.1.call-update
  299.4 0.9 constant_dynamic-slice_fusion
  300.3 0.1 copy.8
  300.4 76.0 %reduce-scatter.5.cloned.1.call-done = f32[256,64]{0,1:T(8,128)} async-done(((f32[256,512]{0,1:T(8,128)}), f32[256,64]{0,1:T(8,128)}) %reduce-scatter.5.cloned.1.call-update) | async-done | bytes 65552 | tf_op jit(solution)/shard_map/reduce_scatter | solution.py:59
  376.4 0.0 copy-done
  376.4 1.5 subtract_convert_fusion
  377.9 34.4 %all_gather.7 = bf16[256,512]{0,1:T(8,128)(2,1)S(1)} all-gather(bf16[256,64]{0,1:T(8,128)(2,1)S(1)} %get-tuple-element.8), channel_id=1, replica_groups=mesh['group'=8,'fsdp'=32] {'group'}, dimensions={1}, use_global_device_ids=true | all-gather | bytes 294912 | tf_op jit(solution)/shard_map/all_gather | solution.py:68
  412.3 0.8 copy.7
  (2 shorter events, 0.0 us)
Async XLA Ops:
  7.2 77.9 %all-gather.2.cloned.1.call-start = ((), (), s32[]{:S(2)}) async-start(), calls=%async_computation.2 | async-start | bytes 8650752 | tf_op jit(solution)/shard_map/all_gather | solution.py:37
  7.9 288.3 %reduce-scatter.3.cloned.1.call-start = ((), (), s32[]{:S(2)}) async-start(), calls=%async_computation.3 | async-start | bytes 17301504 | tf_op jit(solution)/shard_map/reduce_scatter | solution.py:45
  108.1 268.2 %copy-start = (f32[256,64]{0,1:T(8,128)S(1)}, f32[256,64]{0,1:T(8,128)}, u32[]{:S(2)}) copy-start(f32[256,64]{0,1:T(8,128)} %param.7) | copy-start | bytes 196612
  108.2 268.2 %reduce-scatter.5.cloned.1.call-start = ((), (), s32[]{:S(2)}) async-start(), calls=%async_computation.4 | async-start | bytes 589824 | tf_op jit(solution)/shard_map/reduce_scatter | solution.py:59
Sparse Core Ops, SparseCore 0:
  9.9 75.1 all-gather.1
  108.3 187.8 reduce-scatter.2
  300.0 76.2 reduce-scatter.4
where the time goes:
time: 420 us
  waiting for transfers between devices  342 us (81%)
  blocking collectives  34.4 us (8%)
  matrix products  23 us (5%)
  between operations  13.8 us (3%)
  other arithmetic  4.6 us (1%)
    reduce_scatter x1, waiting for transfers between devices, body(): lax.psum_scatter(lax.dot_general(columns, cotangent, (((0,), (0,)), ((),...  188 us
    all_gather x1, waiting for transfers between devices, body(): lax.all_gather(weight, 'fsdp', axis=0, tiled=True)  77.2 us
    reduce_scatter x1, waiting for transfers between devices, body(): lax.psum_scatter(decoded.reshape(shard_rows, out_width), 'group', scatter...  76 us
    all_gather x1, blocking collectives, body(): new_weight = lax.all_gather(updated, 'group', axis=1, tiled=True)  34.4 us
    dot_general x1, matrix products, body(): lax.dot_general(columns, cotangent, (((0,), (0,)), ((), ())), preferred_e...  23 us
  transfers between devices with their start and end apart: 3, of which 3 were waited for; matrix products, arithmetic and copies ran while one was open for 0% of the time, Pallas kernels for 0%

commit v1 on v0

v1 whole, which is shorter than its diff:
```python
import functools
import math

import jax
import jax.numpy as jnp
from jax import lax
from jax.experimental import pallas as pl
from jax.experimental.pallas import tpu as pltpu
from jax.sharding import PartitionSpec as P

BLOCK = 32
inner_rate = 0.5
momentum_decay = 0.9
outer_rate = 0.7

MESH = pl.DeviceIdType.MESH
F32 = jnp.float32
BF16 = jnp.bfloat16

NZ, NX, NC, NY, NH = 8, 2, 2, 4, 2
NG = NY * NH
D, KVW, TOK = 8192, 512, 512
ROWS = D // (NZ * NX * NC)
HALF = ROWS // 2
QUART = ROWS // 4
OWN = KVW // NG
LANES = 128

GATHER = (
    (0, 0), (0, 1), (1, 0), (-1, 0), (1, 1), (-1, 1), (2, 0), (-2, 0),
    (2, 1), (-2, 1), (3, 0), (-3, 0), (3, 1), (-3, 1), (4, 0), (4, 1),
)
INDEX = {o: k for k, o in enumerate(GATHER)}
N = len(GATHER)
SCATTER = (
    (4, 1), (4, 0), (3, 1), (-3, 1), (3, 0), (-3, 0), (1, 1), (-1, 1),
    (0, 1), (2, 1), (-2, 1), (2, 0), (-2, 0), (1, 0), (-1, 0), (0, 0),
)
LAG_FINAL, LAG_CORE = 3, 1


def children(o, s):
    oz, ox = o
    out = []
    if oz == 4:
        return out
    if ox == 0:
        if 0 <= oz < 3 or (oz == 3 and s == 0):
            out.append(("up", (oz + 1, 0)))
        if -3 < oz <= 0 or (oz == -3 and s == 1):
            out.append(("down", (oz - 1 if oz > -3 else 4, 0)))
        if abs(oz) <= 2:
            out.append(("across", (oz, 1)))
    else:
        if oz == 2 or (oz == 3 and s == 0):
            out.append(("up", (oz + 1, 1)))
        if oz == -2 or (oz == -3 and s == 1):
            out.append(("down", (oz - 1 if oz > -3 else 4, 1)))
    return out


REVERSE = {"up": "down", "down": "up", "across": "across"}
PARENT = {(c, s): (REVERSE[d], o) for o in GATHER for s in range(2) for d, c in children(o, s)}


def pick(k, table):
    got = jnp.int32(table[0])
    for at in range(1, len(table)):
        got = jnp.where(k == at, jnp.int32(table[at]), got)
    return got


def kernel(
    tok_hbm, tgt_hbm, w_hbm, mom_hbm, nw_hbm, nm_hbm,
    x_own, x_oth, wfull, acc, tgt, mom, cot_own, cot_par, gbuf, sbuf, rbuf,
    dec, gsum, w_t, m_t, upd, wn_t, nw, nm,
    load_sem, out_sem, send_sem, zx_sem, fin_sem, core_sem, tok_sem, cot_sem, rs_sem, ex_sem, up_sem,
):
    g = lax.axis_index("group")
    f = lax.axis_index("fsdp")
    xh, y = g // NY, g % NY
    z, xl, c = f // (NX * NC), (f // NC) % NX, f % NC

    def at(zz, xx, cc):
        return (zz * NX + xx) * NC + cc

    to = {
        "up": {"group": g, "fsdp": at((z + 1) % NZ, xl, c)},
        "down": {"group": g, "fsdp": at((z + NZ - 1) % NZ, xl, c)},
        "across": {"group": g, "fsdp": at(z, 1 - xl, c)},
        "core": {"group": g, "fsdp": at(z, xl, 1 - c)},
        "y_up": {"group": xh * NY + (y + 1) % NY, "fsdp": f},
        "y_down": {"group": xh * NY + (y + NY - 1) % NY, "fsdp": f},
        "beyond": {"group": (1 - xh) * NY + y, "fsdp": at(z, 1 - xl, c)},
    }

    def send(src, dst, s_sem, r_sem, device):
        copy = pltpu.make_async_remote_copy(
            src_ref=src, dst_ref=dst, send_sem=s_sem, recv_sem=r_sem, device_id=device, device_id_type=MESH
        )
        copy.start()

    def wait(ref, sem):
        pltpu.make_async_copy(ref, ref, sem).wait()

    def chip_of(enc):
        return (z + NZ - enc // 2) % NZ, (xl + enc) % 2

    def shard_of(o):
        zz, xx = chip_of((o[0] % NZ) * 2 + o[1])
        return at(zz, xx, c)

    w_load = pltpu.make_async_copy(w_hbm, wfull.at[pl.ds(pl.multiple_of(f * ROWS, ROWS), ROWS)], load_sem.at[0])
    w_load.start()

    @pl.loop(0, NZ * NX * NC)
    def _(j):
        pltpu.make_async_copy(
            tok_hbm.at[:, pl.ds(pl.multiple_of(j * ROWS, ROWS), ROWS)], x_own.at[j], load_sem.at[1]
        ).start()

    t_load = pltpu.make_async_copy(tgt_hbm, tgt, load_sem.at[2])
    t_load.start()
    m_load = pltpu.make_async_copy(mom_hbm, mom, load_sem.at[3])
    m_load.start()

    barrier = pltpu.get_barrier_semaphore()
    for name in ("up", "down", "across", "core", "beyond"):
        pl.semaphore_signal(barrier, inc=1, device_id=to[name], device_id_type=MESH)
    for step in range(1, NG):
        pl.semaphore_signal(
            barrier, inc=1, device_id={"group": (g + step) % NG, "fsdp": f}, device_id_type=MESH
        )
    pl.semaphore_wait(barrier, 5 + NG - 1)
    w_load.wait()

    mine = pl.multiple_of(((y + xh) % 2) * HALF, HALF)
    theirs = pl.multiple_of(HALF - mine, HALF)

    def rows(shard, start, count):
        return wfull.at[pl.ds(pl.multiple_of(shard * ROWS + start, 16), count)]

    def pass_on(k):
        o = GATHER[k]
        shard = shard_of(o)
        for s in range(2):
            piece = rows(shard, mine + s * QUART, QUART)
            if k > 0:
                wait(piece, zx_sem.at[k, s])
            for direction, child in children(o, s):
                send(piece, piece, send_sem.at[0], zx_sem.at[INDEX[child], s], to[direction])
        if k > 0:
            for name, start, count in (("y_up", 0, 48), ("y_down", 48, 48)):
                piece = rows(shard, mine + start, count)
                send(piece, piece, send_sem.at[0], fin_sem.at[k], to[name])
        if o != (0, 1):
            piece = rows(shard, mine + 96, 32)
            send(piece, piece, send_sem.at[0], fin_sem.at[INDEX[(o[0], 1 - o[1])]], to["beyond"])

    enc_table = [(oz % NZ) * 2 + ox for oz, ox in GATHER]
    acc[...] = jnp.zeros_like(acc)

    @pl.loop(0, N + LAG_FINAL + LAG_CORE)
    def _(t):
        for k in range(N):
            @pl.when(t == k)
            def _(k=k):
                pass_on(k)

        @pl.when(t < N)
        def _():
            shard = t * NC + 1 - c
            send(
                tok_hbm.at[:, pl.ds(pl.multiple_of(shard * ROWS, ROWS), ROWS)],
                x_oth.at[t], send_sem.at[1], tok_sem.at[0], to["core"],
            )

        @pl.when((t >= LAG_FINAL) & (t < N + LAG_FINAL))
        def _():
            k = t - LAG_FINAL
            zz, xx = chip_of(pick(k, enc_table))
            shard = at(zz, xx, c)

            @pl.when(k > 0)
            def _():
                wait(rows(shard, theirs, HALF), fin_sem.at[k])

            piece = rows(shard, 0, ROWS)
            send(piece, piece, send_sem.at[0], core_sem.at[k], to["core"])

        @pl.when(t == LAG_FINAL)
        def _():
            wait(x_own, load_sem.at[1])

        @pl.when(t >= LAG_FINAL + LAG_CORE)
        def _():
            k = t - LAG_FINAL - LAG_CORE
            zz, xx = chip_of(pick(k, enc_table))
            a, b = at(zz, xx, c), at(zz, xx, 1 - c)
            wait(rows(b, 0, ROWS), core_sem.at[k])
            acc[...] += jnp.dot(
                x_own[a], wfull[pl.ds(pl.multiple_of(a * ROWS, ROWS), ROWS), :], preferred_element_type=F32
            ) + jnp.dot(
                x_own[b], wfull[pl.ds(pl.multiple_of(b * ROWS, ROWS), ROWS), :], preferred_element_type=F32
            )

    root_width = math.sqrt(D)
    grad_scale = math.sqrt(D / (TOK * NZ * NX * NC))
    t_load.wait()
    cot = (acc[...] / root_width - tgt[...].astype(F32)) * grad_scale
    cot_own[...] = cot.T.astype(BF16)
    send(cot_own, cot_par, send_sem.at[2], cot_sem.at[0], to["core"])

    m_load.wait()
    w_t[...] = wfull[pl.ds(pl.multiple_of(f * ROWS, ROWS), ROWS), :].astype(F32).T
    m_t[...] = jnp.concatenate([mom[...], jnp.zeros_like(mom)], axis=1).T[:OWN]

    wait(x_oth, tok_sem.at[0])
    wait(cot_par, cot_sem.at[0])

    def leaf(o, s):
        return not children(o, s)

    def send_sum(o, s):
        k = INDEX[o]
        direction, _ = PARENT[o, s]
        send(sbuf.at[k, s], rbuf.at[k, s], send_sem.at[3], rs_sem.at[k, s], to[direction])

    scatter_enc = [(oz % NZ) * 2 + ox for oz, ox in SCATTER]
    scatter_k = [INDEX[o] for o in SCATTER]

    @pl.loop(0, N)
    def _(t):
        zz, xx = chip_of(pick(t, scatter_enc))
        k = pick(t, scatter_k)
        grad = jnp.dot(cot_own[...], x_own[at(zz, xx, c)], preferred_element_type=F32) + jnp.dot(
            cot_par[...], x_oth[zz * NX + xx], preferred_element_type=F32
        )
        for s in range(2):
            gbuf[k, s] = grad[:, s * LANES : (s + 1) * LANES]
            sbuf[k, s] = grad[:, s * LANES : (s + 1) * LANES].astype(BF16)
        for n, o in enumerate(SCATTER):
            if any(leaf(o, s) for s in range(2)):
                @pl.when(t == n)
                def _(o=o):
                    for s in range(2):
                        if leaf(o, s):
                            send_sum(o, s)

    def total(o, s):
        k = INDEX[o]
        got = gbuf[k, s]
        for _, child in children(o, s):
            kc = INDEX[child]
            wait(rbuf.at[kc, s], rs_sem.at[kc, s])
            got = got + rbuf[kc, s].astype(F32)
        return got

    steps = (
        ((3, 1), 0), ((-3, 1), 1), ((2, 1), 1), ((-2, 1), 0), ((3, 0), 0), ((-3, 0), 1),
        ((2, 1), 0), ((-2, 1), 1), ((2, 0), 1), ((-2, 0), 0), ((1, 0), 1), ((-1, 0), 0),
        ((2, 0), 0), ((-2, 0), 1), ((1, 0), 0), ((-1, 0), 1),
    )
    for o, s in steps:
        sbuf[INDEX[o], s] = total(o, s).astype(BF16)
        send_sum(o, s)

    mine_rows = pl.multiple_of(g * OWN, OWN)
    for s in (1, 0):
        delta = (inner_rate * (total((0, 0), s) / root_width)).reshape(KVW // BLOCK, BLOCK, LANES)
        largest = jnp.max(jnp.abs(delta), axis=1, keepdims=True)
        block_scale = jnp.exp2(jnp.ceil(jnp.log2(largest / 6.0 + 1e-30))).astype(BF16).astype(F32)
        code = jnp.clip(delta / block_scale, -6.0, 6.0).astype(BF16)
        dec[s] = (code.astype(F32) * block_scale).reshape(KVW, LANES).astype(BF16)
        for step in range(1, NG):
            other = (g + step) % NG
            send(
                dec.at[s, pl.ds(pl.multiple_of(other * OWN, OWN), OWN)], gsum.at[s, g],
                send_sem.at[4], ex_sem.at[s], {"group": other, "fsdp": f},
            )
        gsum[s, g] = dec[s, pl.ds(mine_rows, OWN), :]

    for s in (1, 0):
        wait(gsum.at[s, pl.ds(0, NG - 1)], ex_sem.at[s])
        summed = gsum[s, 0].astype(F32)
        for step in range(1, NG):
            summed = summed + gsum[s, step].astype(F32)
        average = summed / NG
        lanes = slice(s * LANES, (s + 1) * LANES)
        new_mom = momentum_decay * m_t[:, lanes] + average
        own_w = w_t[pl.ds(mine_rows, OWN), lanes]
        new_w = (own_w - outer_rate * (average + momentum_decay * new_mom)).astype(BF16)
        upd[s] = new_w
        for step in range(1, NG):
            other = (g + step) % NG
            send(
                upd.at[s], wn_t.at[s, pl.ds(mine_rows, OWN)], send_sem.at[5], up_sem.at[s],
                {"group": other, "fsdp": f},
            )
        wn_t[s, pl.ds(mine_rows, OWN), :] = new_w
        nm[s * LANES : (s + 1) * LANES, :] = jnp.concatenate([new_mom, jnp.zeros_like(new_mom)], axis=0).T[:, :OWN]
    nm_out = pltpu.make_async_copy(nm, nm_hbm, out_sem.at[0])
    nm_out.start()

    for s in (1, 0):
        wait(wn_t.at[s, pl.ds(0, KVW - OWN)], up_sem.at[s])
        nw[s * LANES : (s + 1) * LANES, :] = wn_t[s].astype(F32).T.astype(BF16)
    nw_out = pltpu.make_async_copy(nw, nw_hbm, out_sem.at[1])
    nw_out.start()

    wait(wfull.at[pl.ds(0, (N - 1) * ROWS + N * ROWS)], send_sem.at[0])
    wait(x_oth, send_sem.at[1])
    wait(cot_own, send_sem.at[2])
    wait(sbuf.at[pl.ds(0, N - 1)], send_sem.at[3])
    wait(gsum.at[:, pl.ds(0, NG - 1)], send_sem.at[4])
    wait(gsum.at[:, pl.ds(0, NG - 1)], send_sem.at[5])
    nm_out.wait()
    nw_out.wait()


def body(tokens, target, weight, momentum):
    hbm = pl.BlockSpec(memory_space=pl.ANY)
    dma = pltpu.SemaphoreType.DMA
    return pl.pallas_call(
        kernel,
        out_shape=(
            jax.ShapeDtypeStruct((ROWS, KVW), BF16),
            jax.ShapeDtypeStruct((ROWS, OWN), F32),
        ),
        in_specs=[hbm] * 4,
        out_specs=(hbm, hbm),
        scratch_shapes=[
            pltpu.VMEM((NZ * NX * NC, TOK, ROWS), BF16),
            pltpu.VMEM((NZ * NX, TOK, ROWS), BF16),
            pltpu.VMEM((D, KVW), BF16),
            pltpu.VMEM((TOK, KVW), F32),
            pltpu.VMEM((TOK, KVW), BF16),
            pltpu.VMEM((ROWS, OWN), F32),
            pltpu.VMEM((KVW, TOK), BF16),
            pltpu.VMEM((KVW, TOK), BF16),
            pltpu.VMEM((N, 2, KVW, LANES), F32),
            pltpu.VMEM((N, 2, KVW, LANES), BF16),
            pltpu.VMEM((N, 2, KVW, LANES), BF16),
            pltpu.VMEM((2, KVW, LANES), BF16),
            pltpu.VMEM((2, NG, OWN, LANES), BF16),
            pltpu.VMEM((KVW, ROWS), F32),
            pltpu.VMEM((OWN, ROWS), F32),
            pltpu.VMEM((2, OWN, LANES), BF16),
            pltpu.VMEM((2, KVW, LANES), BF16),
            pltpu.VMEM((ROWS, KVW), BF16),
            pltpu.VMEM((ROWS, OWN), F32),
            dma((4,)), dma((2,)), dma((6,)), dma((N, 2)), dma((N,)), dma((N,)), dma((1,)), dma((1,)),
            dma((N, 2)), dma((2,)), dma((2,)),
        ],
        compiler_params=pltpu.CompilerParams(
            collective_id=0, has_side_effects=True, vmem_limit_bytes=56 * 1024 * 1024
        ),
        cost_estimate=pl.CostEstimate(
            flops=4 * TOK * D * KVW, bytes_accessed=2 * TOK * D + 4 * ROWS * KVW, transcendentals=0
        ),
    )(tokens, target, weight, momentum)


def solution(mesh):
    placed = (
        P(("group", "fsdp"), None),
        P(("group", "fsdp"), None),
        P("fsdp", None),
        P("fsdp", "group"),
    )
    return jax.shard_map(
        body,
        mesh=mesh,
        in_specs=placed,
        out_specs=(P("fsdp", None), P("fsdp", "group")),
        check_vma=False,
    )
```

time: 420 us -> 111 us (0.26)
  waiting for transfers between devices: 342 us -> 0 us
  Pallas kernels: 0 us -> 105 us
  blocking collectives: 34.4 us -> 0 us
  matrix products: 23 us -> 0 us
  between operations: 13.8 us -> 0.64 us
  other arithmetic: 4.6 us -> 0 us
    reduce_scatter x2 -> x0, waiting for transfers between devices: 264 us -> none  [the longest x1 188 us: body(): lax.psum_scatter(lax.dot_general(columns, cotangent, (((0,), (0,)), ((),...]
    pallas_call x0 -> x1, Pallas kernels: none -> 105 us  [body(): pl.pallas_call(kernel, out_shape=(jax.ShapeDtypeStruct((ROWS, KVW), BF16)...]
    all_gather x1 -> x0, waiting for transfers between devices: 77.2 us -> none  [body(): lax.all_gather(weight, 'fsdp', axis=0, tiled=True)]
    all_gather x1 -> x0, blocking collectives: 34.4 us -> none  [body(): new_weight = lax.all_gather(updated, 'group', axis=1, tiled=True)]
    dot_general x1 -> x0, matrix products: 23 us -> none  [body(): lax.dot_general(columns, cotangent, (((0,), (0,)), ((), ())), preferred_e...]
  transfers between devices with their start and end apart: 3 -> 0, of which waited for: 3 -> 0; matrix products, arithmetic and copies ran while one was open for 0% -> 0% of each run, Pallas kernels for 0% -> 0%
where the time goes in v1:
time: 111 us
  Pallas kernels  105 us (95%)
  local copies, waits for them, and re-layouts  4.88 us (4%)
    pallas_call x1, Pallas kernels, body(): pl.pallas_call(kernel, out_shape=(jax.ShapeDtypeStruct((ROWS, KVW), BF16)...  105 us
    unnamed x2, local copies, waits for them, and re-layouts  3.26 us

profile of v1, /device:TPU:2, one launch (start us, length us, event | category | flops | bytes accessed | tf_op | source)
XLA Modules:
  0.0 110.6 jit_solution(2973754367330534352)
XLA Ops:
  0.6 1.6 %copy.6.mom_hbm = f32[256,64]{1,0:T(8,128)} copy(f32[256,64]{0,1:T(8,128)} %param.7) | data formatting | bytes 131072 | tf_op args[3]
  2.2 105.1 %shard_map.59 = (bf16[256,512]{1,0:T(8,128)(2,1)}, f32[256,64]{1,0:T(8,128)}) custom-call(bf16[512,8192]{1,0:T(8,128)(2,1)} %tok_hbm.1, bf16[512,512]{1,0:T(8,128)(2,1)} %tgt_hbm.1, bf16[256,512]{1,0:T(8,128)(2,1)} %w_hbm.1, f32[256,64]{1,0:T(8,128)} %copy.6.mom_hbm), custom_call_target="tpu_custom_call" | custom-call | flops 8589934592 | bytes 8912896 | tf_op jit(solution)/shard_map/pallas_call | solution.py:324
  107.3 1.6 %copy.7 = f32[256,64]{0,1:T(8,128)} copy(f32[256,64]{1,0:T(8,128)} %get-tuple-element.3) | data formatting | bytes 131072 | tf_op jit(solution)/shard_map/pallas_call | solution.py:324
  109.0 1.7 %copy.9 = bf16[256,512]{1,0:T(8,128)(2,1)} copy(bf16[256,512]{1,0:T(8,128)(2,1)} %get-tuple-element.6) | data formatting | bytes 524288

commit v2 on v0

v2 whole, which is shorter than its diff:
```python
import math

import jax
import jax.numpy as jnp
from jax import lax
from jax.experimental import pallas as pl
from jax.experimental.pallas import tpu as pltpu
from jax.sharding import PartitionSpec as P

BLOCK = 32
inner_rate = 0.5
momentum_decay = 0.9
outer_rate = 0.7

MESH = pl.DeviceIdType.MESH
F32 = jnp.float32
BF16 = jnp.bfloat16

NZ, NX, NC, NY, NH = 8, 2, 2, 4, 2
NG = NY * NH
D, KVW, TOK = 8192, 512, 512
ROWS = D // (NZ * NX * NC)
HALF = ROWS // 2
OWN = KVW // NG
LANES = 128
QG, QR = 2, 2
PIECE = HALF // 2 // QG
PART = KVW // QR

GATHER_ACROSS = (-3, -2, 0, 1, 2)
SPLITS = (((32, 16, 16), (16, 32, 16)), ((32, 16, 16), (16, 16, 32)), ((16, 32, 16), (16, 16, 32)))
SPLIT_AT = (2, 1, 2, 0, 0, 1, 2, 0)
GATHER = (
    ("s", -1, 0, 1, 0), ("s", -1, 0, 1, 1), ("s", 1, 0, 0, 0), ("s", 1, 0, 0, 1), ("s", 1, 0, 1, 0),
    ("s", 0, 1, 0, 0), ("f", 0, 0, 0), ("f", 0, 0, 1), ("s", 0, 1, 0, 1), ("s", 0, 1, 1, 0), ("s", -1, 0, 0, 0),
    ("c", 0, 0), ("s", -1, 0, 0, 1), ("s", 1, 0, 1, 1), ("s", 0, 1, 1, 1), ("s", -2, 0, 1, 0), ("s", -1, 1, 1, 0),
    ("s", 2, 0, 0, 0), ("s", 1, 1, 0, 0), ("s", -1, 1, 0, 0), ("s", -2, 0, 1, 1), ("f", -1, 0, 1),
    ("s", 2, 0, 0, 1), ("f", 1, 0, 0), ("s", 1, 1, 0, 1), ("s", -1, 1, 0, 1), ("f", 0, 1, 0), ("s", -1, 1, 1, 1),
    ("s", -2, 0, 0, 0), ("s", 2, 0, 1, 0), ("s", 1, 1, 1, 0), ("f", -1, 0, 0), ("s", 2, 0, 1, 1), ("f", 1, 0, 1),
    ("s", -2, 0, 0, 1), ("s", 1, 1, 1, 1), ("f", 0, 1, 1), ("s", -2, 1, 1, 0), ("s", -3, 0, 1, 0),
    ("s", 2, 1, 0, 0), ("s", 3, 0, 0, 0), ("s", 2, 1, 0, 1), ("f", 2, 0, 0), ("s", 3, 0, 0, 1), ("f", -2, 0, 1),
    ("s", -2, 1, 1, 1), ("s", -3, 0, 1, 1), ("s", 3, 0, 1, 0), ("s", 2, 1, 1, 0), ("f", 1, 1, 0), ("f", -1, 1, 0),
    ("f", -1, 1, 1), ("d", 0, 0), ("s", -3, 1, 1, 0), ("s", 3, 0, 1, 1), ("f", 2, 0, 1), ("f", -2, 0, 0),
    ("f", 1, 1, 1), ("s", 2, 1, 1, 1), ("s", -3, 0, 0, 0), ("s", -3, 0, 0, 1), ("s", -2, 1, 0, 0),
    ("s", 4, 0, 1, 0), ("s", -2, 1, 0, 1), ("s", 3, 1, 0, 0), ("s", 4, 0, 0, 0), ("c", 0, 1), ("f", 2, 1, 0),
    ("s", 3, 1, 0, 1), ("f", -3, 0, 1), ("f", 3, 0, 0), ("s", 4, 0, 0, 1), ("s", 4, 0, 1, 1), ("f", -2, 1, 1),
    ("s", -3, 1, 1, 1), ("s", 3, 1, 1, 0), ("d", 0, 1), ("s", 4, 1, 1, 0), ("c", -1, 1), ("f", 3, 0, 1),
    ("c", -1, 0), ("s", 3, 1, 1, 1), ("s", -3, 1, 0, 0), ("f", 2, 1, 1), ("s", 4, 1, 0, 0), ("c", 1, 1),
    ("s", -3, 1, 0, 1), ("f", -3, 0, 0), ("d", -1, 1), ("f", -2, 1, 0), ("c", 1, 0), ("s", 4, 1, 0, 1),
    ("f", 3, 1, 0), ("d", -1, 0), ("f", 4, 0, 1), ("s", 4, 1, 1, 1), ("f", 4, 0, 0), ("f", 3, 1, 1),
    ("f", -3, 1, 1), ("c", 2, 1), ("d", 1, 0), ("d", 1, 1), ("f", -3, 1, 0), ("f", 4, 1, 0), ("c", -2, 1),
    ("c", 2, 0), ("d", 2, 1), ("f", 4, 1, 1), ("c", -2, 0), ("d", -2, 1), ("c", 3, 0), ("d", 2, 0), ("c", 3, 1),
    ("d", -2, 0), ("c", -3, 1), ("c", -3, 0), ("d", 3, 0), ("c", 4, 1), ("d", 3, 1), ("c", 4, 0), ("d", -3, 1),
    ("d", -3, 0), ("d", 4, 1), ("d", 4, 0),
)

SUM_ACROSS = (-2, -1, 0, 1, 2)
SUM = (
    ("u", 1, 1), ("p", 1, 1, 0, 0), ("p", 1, 1, 0, 1), ("u", 4, 1), ("p", 4, 1, 0, 0), ("p", 4, 1, 1, 0),
    ("p", 4, 1, 0, 1), ("p", 4, 1, 1, 1), ("u", 2, 0), ("u", -1, 0), ("p", 1, 1, 1, 0), ("u", 3, 1),
    ("p", 3, 1, 1, 0), ("u", -3, 1), ("p", -3, 1, 0, 0), ("u", -2, 1), ("p", 1, 1, 1, 1), ("u", 4, 0),
    ("p", 4, 0, 0, 0), ("p", 4, 0, 1, 0), ("u", -1, 1), ("u", 1, 0), ("p", -1, 1, 0, 0), ("u", -3, 0),
    ("p", 3, 1, 0, 0), ("p", -3, 1, 1, 0), ("u", 0, 0), ("p", -1, 1, 1, 0), ("u", 2, 1), ("u", 0, 1),
    ("p", 3, 1, 0, 1), ("p", -3, 1, 1, 1), ("u", 3, 0), ("p", 2, 1, 1, 0), ("u", -2, 0), ("p", 4, 0, 0, 1),
    ("p", 4, 0, 1, 1), ("p", -2, 1, 0, 0), ("p", 3, 1, 1, 1), ("p", -3, 0, 1, 0), ("p", -2, 1, 1, 0),
    ("p", 3, 0, 1, 0), ("p", -3, 0, 0, 0), ("p", -2, 1, 1, 1), ("p", 3, 0, 1, 1), ("p", -3, 1, 0, 1),
    ("p", 2, 1, 0, 0), ("p", 3, 0, 0, 0), ("p", -3, 0, 1, 1), ("p", 2, 1, 1, 1), ("p", 3, 0, 0, 1),
    ("p", -3, 0, 0, 1), ("p", 2, 1, 0, 1), ("p", 2, 0, 1, 0), ("p", -2, 0, 1, 0), ("p", -2, 1, 0, 1),
    ("p", -2, 0, 0, 0), ("p", 2, 0, 0, 0), ("p", -1, 1, 0, 1), ("p", -2, 0, 1, 1), ("p", 2, 0, 1, 1),
    ("p", -1, 1, 1, 1), ("p", 2, 0, 0, 1), ("p", -1, 0, 1, 0), ("p", 0, 1, 1, 0), ("p", 1, 0, 1, 0),
    ("p", -2, 0, 0, 1), ("p", 0, 1, 0, 0), ("p", 1, 0, 0, 0), ("p", -1, 0, 0, 0), ("p", 0, 1, 1, 1),
    ("p", 1, 0, 1, 1), ("p", -1, 0, 1, 1), ("p", 0, 1, 0, 1), ("p", 1, 0, 0, 1), ("p", 0, 0, 1, 0),
    ("p", -1, 0, 0, 1), ("p", 0, 0, 0, 0), ("p", 0, 0, 1, 1), ("p", 0, 0, 0, 1),
)

OFFSETS = tuple((oz, ox) for ox in range(2) for oz in (0, 1, -1, 2, -2, 3, -3, 4))
INDEX = {o: k for k, o in enumerate(OFFSETS)}
N = len(OFFSETS)
REVERSE = {"up": "down", "down": "up", "across": "across"}


def tree(across):
    parent = {}
    for s in range(2):
        sign = 1 if s == 0 else -1

        def real(oz, sign=sign):
            return 4 if oz == 4 else oz * sign

        for oz in range(-3, 5):
            step = 1 if oz > 0 else -1
            hop = ("up" if step * sign > 0 else "down", real(oz - step))
            if oz != 0:
                parent[(real(oz), 0), s] = (hop[0], (hop[1], 0))
            if oz in across:
                parent[(real(oz), 1), s] = ("across", (real(oz), 0))
            else:
                parent[(real(oz), 1), s] = (hop[0], (hop[1], 1))
    return parent


GATHER_TREE = tree(GATHER_ACROSS)
SUM_TREE = tree(SUM_ACROSS)


def children(o, s):
    return [c for (c, r), (_, p) in SUM_TREE.items() if (p, r) == (o, s)]


def pick(k, table):
    got = jnp.int32(table[0])
    for at in range(1, len(table)):
        got = jnp.where(k == at, jnp.int32(table[at]), got)
    return got


def encoded(offsets):
    return [(oz % NZ) * 2 + ox for oz, ox in offsets]


def kernel(
    tok_hbm, tgt_hbm, w_hbm, mom_hbm, nw_hbm, nm_hbm,
    x_own, x_oth, wfull, acc, tgt, mom, cot_own, cot_par, gbuf, sbuf, rbuf,
    dec, gsum, w_t, upd, nm,
    load_sem, out_sem, send_sem, zx_sem, fin_sem, core_sem, tok_sem, cot_sem, rs_sem, ex_sem, up_sem,
):
    g = lax.axis_index("group")
    f = lax.axis_index("fsdp")
    xh, y = g // NY, g % NY
    z, xl, c = f // (NX * NC), (f // NC) % NX, f % NC

    def at(zz, xx, cc):
        return (zz * NX + xx) * NC + cc

    to = {
        "up": {"group": g, "fsdp": at((z + 1) % NZ, xl, c)},
        "down": {"group": g, "fsdp": at((z + NZ - 1) % NZ, xl, c)},
        "across": {"group": g, "fsdp": at(z, 1 - xl, c)},
        "core": {"group": g, "fsdp": at(z, xl, 1 - c)},
        "y_up": {"group": xh * NY + (y + 1) % NY, "fsdp": f},
        "y_down": {"group": xh * NY + (y + NY - 1) % NY, "fsdp": f},
        "beyond": {"group": (1 - xh) * NY + y, "fsdp": at(z, 1 - xl, c)},
    }

    barrier = pltpu.get_barrier_semaphore()
    for name in to:
        pl.semaphore_signal(barrier, inc=1, device_id=to[name], device_id_type=MESH)

    def send(src, dst, s_sem, r_sem, device):
        pltpu.make_async_remote_copy(
            src_ref=src, dst_ref=dst, send_sem=s_sem, recv_sem=r_sem, device_id=device, device_id_type=MESH
        ).start()

    def wait(ref, sem):
        pltpu.make_async_copy(ref, ref, sem).wait()

    def chip_of(enc):
        return (z + NZ - enc // 2) % NZ, (xl + enc) % 2

    def shard_of(o):
        zz, xx = chip_of((o[0] % NZ) * 2 + o[1])
        return at(zz, xx, c)

    w_load = pltpu.make_async_copy(w_hbm, wfull.at[pl.ds(pl.multiple_of(f * ROWS, ROWS), ROWS)], load_sem.at[0])
    w_load.start()

    @pl.loop(0, NZ * NX * NC)
    def _(j):
        pltpu.make_async_copy(
            tok_hbm.at[:, pl.ds(pl.multiple_of(j * ROWS, ROWS), ROWS)], x_own.at[j], load_sem.at[1]
        ).start()

    t_load = pltpu.make_async_copy(tgt_hbm, tgt, load_sem.at[2])
    t_load.start()
    m_load = pltpu.make_async_copy(mom_hbm, mom, load_sem.at[3])
    m_load.start()

    pl.semaphore_wait(barrier, len(to))

    mine = pl.multiple_of(((y + xh) % 2) * HALF, HALF)
    theirs = pl.multiple_of(HALF - mine, HALF)

    def rows(o, start, count):
        return wfull.at[pl.ds(pl.multiple_of(shard_of(o) * ROWS + start, 16), count)]

    def source(o, start, count):
        return w_hbm.at[pl.ds(pl.multiple_of(start, 16), count)] if o == (0, 0) else rows(o, start, count)

    arrived = set()

    def have(o, s, q):
        if o != (0, 0) and (o, s, q) not in arrived:
            arrived.add((o, s, q))
            wait(rows(o, mine + (s * QG + q) * PIECE, PIECE), zx_sem.at[INDEX[o], s, q])

    def gather_op(op):
        kind, o = op[0], (op[1], op[2])
        k = INDEX[o]
        if kind == "s":
            s, q = op[3:]
            direction, before = GATHER_TREE[o, s]
            have(before, s, q)
            start = mine + (s * QG + q) * PIECE
            send(
                source(before, start, PIECE), rows(before, start, PIECE),
                send_sem.at[0], zx_sem.at[k, s, q], to[direction],
            )
        elif kind == "f":
            s = op[3]
            for q in range(QG):
                have(o, s, q)
            start = mine + s * (HALF // 2)
            for name, count in zip(("y_up", "y_down", "beyond"), SPLITS[SPLIT_AT[o[0] % NZ]][s]):
                there = (o[0], 1 - o[1]) if name == "beyond" else o
                if there != (0, 0):
                    send(
                        source(o, start, count), rows(o, start, count),
                        send_sem.at[0], fin_sem.at[INDEX[there]], to[name],
                    )
                start = start + count
        elif kind == "c":
            if o != (0, 0):
                wait(rows(o, theirs, HALF), fin_sem.at[k])
            send(source(o, 0, ROWS), rows(o, 0, ROWS), send_sem.at[0], core_sem.at[k], to["core"])

    first = next(n for n, op in enumerate(GATHER) if op[0] == "f")
    for op in GATHER[:first]:
        gather_op(op)

    @pl.loop(0, N)
    def _(j):
        send(
            tok_hbm.at[:, pl.ds(pl.multiple_of((j * NC + 1 - c) * ROWS, ROWS), ROWS)],
            x_oth.at[j], send_sem.at[1], tok_sem.at[0], to["core"],
        )

    acc[...] = jnp.zeros_like(acc)
    groups, order = [[]], []
    for op in GATHER[first:]:
        if op[0] == "d":
            order.append((op[1], op[2]))
            groups.append([])
        else:
            groups[-1].append(op)

    @pl.loop(0, N)
    def _(t):
        for n in range(N):
            if groups[n]:
                @pl.when(t == n)
                def _(n=n):
                    for op in groups[n]:
                        gather_op(op)

        @pl.when(t == 0)
        def _():
            w_load.wait()
            wait(x_own, load_sem.at[1])

        zz, xx = chip_of(pick(t, encoded(order)))
        k = pick(t, [INDEX[o] for o in order])
        a, b = at(zz, xx, c), at(zz, xx, 1 - c)
        rows_a = pl.ds(pl.multiple_of(a * ROWS, ROWS), ROWS)
        rows_b = pl.ds(pl.multiple_of(b * ROWS, ROWS), ROWS)
        wait(wfull.at[rows_b], core_sem.at[k])
        acc[...] += jnp.dot(x_own[a], wfull[rows_a, :], preferred_element_type=F32) + jnp.dot(
            x_own[b], wfull[rows_b, :], preferred_element_type=F32
        )

    root_width = math.sqrt(D)
    grad_scale = math.sqrt(D / (TOK * NZ * NX * NC))
    t_load.wait()
    for h in range(2):
        toks = slice(h * (TOK // 2), (h + 1) * (TOK // 2))
        cot = (acc[toks, :] / root_width - tgt[toks, :].astype(F32)) * grad_scale
        cot_own[h] = cot.T.astype(BF16)
        send(cot_own.at[h], cot_par.at[h], send_sem.at[2], cot_sem.at[0], to["core"])

    w_t[...] = wfull[pl.ds(pl.multiple_of(f * ROWS, ROWS), ROWS), :].astype(F32).T
    wait(x_oth, tok_sem.at[0])
    wait(cot_par, cot_sem.at[0])

    def total(o, s, q):
        part = pl.ds(q * PART, PART)
        got = gbuf[INDEX[o], s, part, :]
        for child in children(o, s):
            kc = INDEX[child]
            wait(rbuf.at[kc, s, part], rs_sem.at[kc, s, q])
            got = got + rbuf[kc, s, part, :].astype(F32)
        return got

    def owner_part(s, q):
        part = pl.ds(q * PART, PART)
        delta = (inner_rate * (total((0, 0), s, q) / root_width)).reshape(PART // BLOCK, BLOCK, LANES)
        largest = jnp.max(jnp.abs(delta), axis=1, keepdims=True)
        block_scale = jnp.exp2(jnp.ceil(jnp.log2(largest / 6.0 + 1e-30))).astype(BF16).astype(F32)
        code = jnp.clip(delta / block_scale, -6.0, 6.0).astype(BF16)
        dec[s, part, :] = (code.astype(F32) * block_scale).reshape(PART, LANES).astype(BF16)
        for j in range(q * PART // OWN, (q + 1) * PART // OWN):
            @pl.when(g != j)
            def _(j=j):
                send(
                    dec.at[s, pl.ds(j * OWN, OWN)], gsum.at[s, g],
                    send_sem.at[4], ex_sem.at[s], {"group": j, "fsdp": f},
                )

            @pl.when(g == j)
            def _(j=j):
                gsum[s, g] = dec[s, pl.ds(j * OWN, OWN), :]

    def sum_op(op):
        o, s, q = (op[1], op[2]), op[3], op[4]
        if o == (0, 0):
            owner_part(s, q)
            return
        k, part = INDEX[o], pl.ds(q * PART, PART)
        if children(o, s):
            sbuf[k, s, part, :] = total(o, s, q).astype(BF16)
        send(
            sbuf.at[k, s, part], rbuf.at[k, s, part],
            send_sem.at[3], rs_sem.at[k, s, q], to[REVERSE[SUM_TREE[o, s][0]]],
        )

    sum_groups, sum_order = [[]], []
    for op in SUM:
        if op[0] == "u":
            sum_order.append((op[1], op[2]))
            sum_groups.append([])
        else:
            sum_groups[-1].append(op)

    @pl.loop(0, N)
    def _(t):
        zz, xx = chip_of(pick(t, encoded(sum_order)))
        k = pick(t, [INDEX[o] for o in sum_order])
        x_a, x_b = x_own[at(zz, xx, c)], x_oth[zz * NX + xx]
        half = TOK // 2
        grad = jnp.dot(cot_own[0], x_a[:half], preferred_element_type=F32)
        grad += jnp.dot(cot_own[1], x_a[half:], preferred_element_type=F32)
        grad += jnp.dot(cot_par[0], x_b[:half], preferred_element_type=F32)
        grad += jnp.dot(cot_par[1], x_b[half:], preferred_element_type=F32)
        for s in range(2):
            gbuf[k, s] = grad[:, s * LANES : (s + 1) * LANES]
            sbuf[k, s] = grad[:, s * LANES : (s + 1) * LANES].astype(BF16)
        for n in range(N - 1):
            if sum_groups[n + 1]:
                @pl.when(t == n)
                def _(n=n):
                    for op in sum_groups[n + 1]:
                        sum_op(op)

    for op in sum_groups[N]:
        sum_op(op)

    m_load.wait()
    mine_rows = pl.multiple_of(g * OWN, OWN)
    tail = [op[3] for op in SUM if op[0] == "p" and (op[1], op[2]) == (0, 0)]
    turn = (1 - tail[-1], tail[-1])
    for s in turn:
        wait(gsum.at[s, pl.ds(0, NG - 1)], ex_sem.at[s])
        summed = gsum[s, 0].astype(F32)
        for step in range(1, NG):
            summed = summed + gsum[s, step].astype(F32)
        average = summed / NG
        lanes = slice(s * LANES, (s + 1) * LANES)
        new_mom = momentum_decay * mom[:, lanes] + average
        own_w = w_t[pl.ds(mine_rows, OWN), lanes]
        upd[s] = (own_w - outer_rate * (average + momentum_decay * new_mom)).astype(BF16)
        for step in range(1, NG):
            send(
                upd.at[s], nw_hbm.at[pl.ds(mine_rows, OWN), pl.ds(s * LANES, LANES)], send_sem.at[5], up_sem.at[0],
                {"group": (g + step) % NG, "fsdp": f},
            )
        pltpu.make_async_copy(
            upd.at[s], nw_hbm.at[pl.ds(mine_rows, OWN), pl.ds(s * LANES, LANES)], out_sem.at[1]
        ).start()
        nm[:, lanes] = new_mom
    nm_out = pltpu.make_async_copy(nm, nm_hbm, out_sem.at[0])
    nm_out.start()

    wait(wfull.at[pl.ds(0, (N - 1) * ROWS + N * ROWS)], send_sem.at[0])
    wait(x_oth, send_sem.at[1])
    wait(cot_own, send_sem.at[2])
    wait(sbuf.at[pl.ds(0, N - 1)], send_sem.at[3])
    wait(gsum.at[:, pl.ds(0, NG - 1)], send_sem.at[4])
    wait(gsum.at[:, pl.ds(0, NG - 1)], send_sem.at[5])
    nm_out.wait()
    wait(upd, out_sem.at[1])
    wait(gsum.at[:, pl.ds(0, NG - 1)], up_sem.at[0])


def finish(nw_t, nm_t, nw, nm):
    nw[...] = nw_t[...].astype(F32).T.astype(BF16)
    nm[...] = nm_t[...]


def body(tokens, target, weight, momentum):
    hbm = pl.BlockSpec(memory_space=pl.ANY)
    dma = pltpu.SemaphoreType.DMA
    nw_t, nm_t = pl.pallas_call(
        kernel,
        out_shape=(
            jax.ShapeDtypeStruct((KVW, ROWS), BF16),
            jax.ShapeDtypeStruct((OWN, ROWS), F32),
        ),
        in_specs=[hbm] * 4,
        out_specs=(hbm, hbm),
        scratch_shapes=[
            pltpu.VMEM((NZ * NX * NC, TOK, ROWS), BF16),
            pltpu.VMEM((N, TOK, ROWS), BF16),
            pltpu.VMEM((D, KVW), BF16),
            pltpu.VMEM((TOK, KVW), F32),
            pltpu.VMEM((TOK, KVW), BF16),
            pltpu.VMEM((OWN, ROWS), F32),
            pltpu.VMEM((2, KVW, TOK // 2), BF16),
            pltpu.VMEM((2, KVW, TOK // 2), BF16),
            pltpu.VMEM((N, 2, KVW, LANES), F32),
            pltpu.VMEM((N, 2, KVW, LANES), BF16),
            pltpu.VMEM((N, 2, KVW, LANES), BF16),
            pltpu.VMEM((2, KVW, LANES), BF16),
            pltpu.VMEM((2, NG, OWN, LANES), BF16),
            pltpu.VMEM((KVW, ROWS), F32),
            pltpu.VMEM((2, OWN, LANES), BF16),
            pltpu.VMEM((OWN, ROWS), F32),
            dma((4,)), dma((2,)), dma((6,)), dma((N, 2, QG)), dma((N,)), dma((N,)), dma((1,)), dma((1,)),
            dma((N, 2, QR)), dma((2,)), dma((1,)),
        ],
        compiler_params=pltpu.CompilerParams(
            collective_id=0, has_side_effects=True, vmem_limit_bytes=56 * 1024 * 1024
        ),
        cost_estimate=pl.CostEstimate(
            flops=4 * TOK * D * KVW, bytes_accessed=2 * TOK * D + 4 * ROWS * KVW, transcendentals=0
        ),
    )(tokens, target, weight, momentum.T)
    new_weight, new_momentum_t = pl.pallas_call(
        finish,
        out_shape=(
            jax.ShapeDtypeStruct((ROWS, KVW), BF16),
            jax.ShapeDtypeStruct((OWN, ROWS), F32),
        ),
    )(nw_t, nm_t)
    return (new_weight, new_momentum_t.T)


def solution(mesh):
    placed = (
        P(("group", "fsdp"), None),
        P(("group", "fsdp"), None),
        P("fsdp", None),
        P("fsdp", "group"),
    )
    return jax.shard_map(
        body,
        mesh=mesh,
        in_specs=placed,
        out_specs=(P("fsdp", None), P("fsdp", "group")),
        check_vma=False,
    )
```

time: 420 us -> 82.1 us (0.20)
  waiting for transfers between devices: 342 us -> 0 us
  Pallas kernels: 0 us -> 80.9 us
  blocking collectives: 34.4 us -> 0 us
  matrix products: 23 us -> 0 us
  between operations: 13.8 us -> 0.64 us
  other arithmetic: 4.6 us -> 0 us
    reduce_scatter x2 -> x0, waiting for transfers between devices: 264 us -> none  [the longest x1 188 us: body(): lax.psum_scatter(lax.dot_general(columns, cotangent, (((0,), (0,)), ((),...]
    pallas_call x0 -> x2, Pallas kernels: none -> 80.9 us  [the longest x1 79.1 us: body(): pl.pallas_call(kernel, out_shape=(jax.ShapeDtypeStruct((KVW, ROWS), BF16)...]
    all_gather x1 -> x0, waiting for transfers between devices: 77.2 us -> none  [body(): lax.all_gather(weight, 'fsdp', axis=0, tiled=True)]
    all_gather x1 -> x0, blocking collectives: 34.4 us -> none  [body(): new_weight = lax.all_gather(updated, 'group', axis=1, tiled=True)]
    dot_general x1 -> x0, matrix products: 23 us -> none  [body(): lax.dot_general(columns, cotangent, (((0,), (0,)), ((), ())), preferred_e...]
  transfers between devices with their start and end apart: 3 -> 0, of which waited for: 3 -> 0; matrix products, arithmetic and copies ran while one was open for 0% -> 0% of each run, Pallas kernels for 0% -> 0%
where the time goes in v2:
time: 82.1 us; the launch traced here: 81.5 us
  Pallas kernels  80.9 us (99%)
    pallas_call x1, Pallas kernels, body(): pl.pallas_call(kernel, out_shape=(jax.ShapeDtypeStruct((KVW, ROWS), BF16)...  79.1 us
    pallas_call x1, Pallas kernels, body(): pl.pallas_call(finish, out_shape=(jax.ShapeDtypeStruct((ROWS, KVW), BF16)...  1.8 us

profile of v2, /device:TPU:2, one launch (start us, length us, event | category | flops | bytes accessed | tf_op | source)
XLA Modules:
  0.0 81.5 jit_solution(13495258511451264905)
XLA Ops:
  0.6 79.1 %shard_map.59 = (bf16[512,256]{1,0:T(8,128)(2,1)}, f32[64,256]{1,0:T(8,128)}) custom-call(bf16[512,8192]{1,0:T(8,128)(2,1)} %tok_hbm.1, bf16[512,512]{1,0:T(8,128)(2,1)} %tgt_hbm.1, bf16[256,512]{1,0:T(8,128)(2,1)} %w_hbm.1, f32[64,256]{1,0:T(8,128)} %bitcast.2), custom_call_target="tpu_custom_call" | custom-call | flops 8589934592 | bytes 8912896 | tf_op jit(solution)/shard_map/pallas_call | solution.py:400
  79.7 1.8 %shard_map.60 = (bf16[256,512]{1,0:T(8,128)(2,1)}, f32[64,256]{1,0:T(8,128)}) custom-call(bf16[512,256]{1,0:T(8,128)(2,1)} %get-tuple-element.6.nw_t, f32[64,256]{1,0:T(8,128)} %get-tuple-element.7.nm_t), custom_call_target="tpu_custom_call" | custom-call | tf_op jit(solution)/shard_map/pallas_call | solution.py:435

commit v3 on v2

--- a/solution.py
+++ b/solution.py
@@ -26,32 +26,40 @@
 QG, QR = 2, 2
 PIECE = HALF // 2 // QG
 PART = KVW // QR
-
-GATHER_ACROSS = (-3, -2, 0, 1, 2)
-SPLITS = (((32, 16, 16), (16, 32, 16)), ((32, 16, 16), (16, 16, 32)), ((16, 32, 16), (16, 16, 32)))
-SPLIT_AT = (2, 1, 2, 0, 0, 1, 2, 0)
+WIDTH = OWN // QR
+
+GATHER_ACROSS = (-2, -1, 0, 1, 3, 4)
+SPLIT = {
+    (-3, 0, 0): (0, 64, 0), (-3, 0, 1): (16, 48, 0), (-3, 1, 0): (0, 64, 0), (-3, 1, 1): (64, 0, 0),
+    (-2, 0, 0): (64, 0, 0), (-2, 0, 1): (48, 16, 0), (-2, 1, 0): (0, 0, 64), (-2, 1, 1): (64, 0, 0),
+    (-1, 0, 0): (16, 48, 0), (-1, 0, 1): (32, 32, 0), (-1, 1, 0): (16, 32, 16), (-1, 1, 1): (16, 16, 32),
+    (0, 0, 0): (64, 0, 0), (0, 0, 1): (32, 32, 0), (0, 1, 0): (16, 16, 32), (0, 1, 1): (32, 16, 16),
+    (1, 0, 0): (32, 16, 16), (1, 0, 1): (32, 32, 0), (1, 1, 0): (32, 16, 16), (1, 1, 1): (0, 0, 64),
+    (2, 0, 0): (16, 48, 0), (2, 0, 1): (16, 48, 0), (2, 1, 0): (0, 0, 64), (2, 1, 1): (0, 0, 64),
+    (3, 0, 0): (32, 32, 0), (3, 0, 1): (32, 32, 0), (3, 1, 0): (0, 0, 64), (3, 1, 1): (0, 0, 64),
+    (4, 0, 0): (32, 32, 0), (4, 0, 1): (32, 32, 0), (4, 1, 0): (0, 0, 64), (4, 1, 1): (0, 0, 64),
+}
 GATHER = (
-    ("s", -1, 0, 1, 0), ("s", -1, 0, 1, 1), ("s", 1, 0, 0, 0), ("s", 1, 0, 0, 1), ("s", 1, 0, 1, 0),
-    ("s", 0, 1, 0, 0), ("f", 0, 0, 0), ("f", 0, 0, 1), ("s", 0, 1, 0, 1), ("s", 0, 1, 1, 0), ("s", -1, 0, 0, 0),
-    ("c", 0, 0), ("s", -1, 0, 0, 1), ("s", 1, 0, 1, 1), ("s", 0, 1, 1, 1), ("s", -2, 0, 1, 0), ("s", -1, 1, 1, 0),
-    ("s", 2, 0, 0, 0), ("s", 1, 1, 0, 0), ("s", -1, 1, 0, 0), ("s", -2, 0, 1, 1), ("f", -1, 0, 1),
-    ("s", 2, 0, 0, 1), ("f", 1, 0, 0), ("s", 1, 1, 0, 1), ("s", -1, 1, 0, 1), ("f", 0, 1, 0), ("s", -1, 1, 1, 1),
-    ("s", -2, 0, 0, 0), ("s", 2, 0, 1, 0), ("s", 1, 1, 1, 0), ("f", -1, 0, 0), ("s", 2, 0, 1, 1), ("f", 1, 0, 1),
-    ("s", -2, 0, 0, 1), ("s", 1, 1, 1, 1), ("f", 0, 1, 1), ("s", -2, 1, 1, 0), ("s", -3, 0, 1, 0),
-    ("s", 2, 1, 0, 0), ("s", 3, 0, 0, 0), ("s", 2, 1, 0, 1), ("f", 2, 0, 0), ("s", 3, 0, 0, 1), ("f", -2, 0, 1),
-    ("s", -2, 1, 1, 1), ("s", -3, 0, 1, 1), ("s", 3, 0, 1, 0), ("s", 2, 1, 1, 0), ("f", 1, 1, 0), ("f", -1, 1, 0),
-    ("f", -1, 1, 1), ("d", 0, 0), ("s", -3, 1, 1, 0), ("s", 3, 0, 1, 1), ("f", 2, 0, 1), ("f", -2, 0, 0),
-    ("f", 1, 1, 1), ("s", 2, 1, 1, 1), ("s", -3, 0, 0, 0), ("s", -3, 0, 0, 1), ("s", -2, 1, 0, 0),
-    ("s", 4, 0, 1, 0), ("s", -2, 1, 0, 1), ("s", 3, 1, 0, 0), ("s", 4, 0, 0, 0), ("c", 0, 1), ("f", 2, 1, 0),
-    ("s", 3, 1, 0, 1), ("f", -3, 0, 1), ("f", 3, 0, 0), ("s", 4, 0, 0, 1), ("s", 4, 0, 1, 1), ("f", -2, 1, 1),
-    ("s", -3, 1, 1, 1), ("s", 3, 1, 1, 0), ("d", 0, 1), ("s", 4, 1, 1, 0), ("c", -1, 1), ("f", 3, 0, 1),
-    ("c", -1, 0), ("s", 3, 1, 1, 1), ("s", -3, 1, 0, 0), ("f", 2, 1, 1), ("s", 4, 1, 0, 0), ("c", 1, 1),
-    ("s", -3, 1, 0, 1), ("f", -3, 0, 0), ("d", -1, 1), ("f", -2, 1, 0), ("c", 1, 0), ("s", 4, 1, 0, 1),
-    ("f", 3, 1, 0), ("d", -1, 0), ("f", 4, 0, 1), ("s", 4, 1, 1, 1), ("f", 4, 0, 0), ("f", 3, 1, 1),
-    ("f", -3, 1, 1), ("c", 2, 1), ("d", 1, 0), ("d", 1, 1), ("f", -3, 1, 0), ("f", 4, 1, 0), ("c", -2, 1),
-    ("c", 2, 0), ("d", 2, 1), ("f", 4, 1, 1), ("c", -2, 0), ("d", -2, 1), ("c", 3, 0), ("d", 2, 0), ("c", 3, 1),
-    ("d", -2, 0), ("c", -3, 1), ("c", -3, 0), ("d", 3, 0), ("c", 4, 1), ("d", 3, 1), ("c", 4, 0), ("d", -3, 1),
-    ("d", -3, 0), ("d", 4, 1), ("d", 4, 0),
+    ("s", -1, 0, 1, 0), ("s", 0, 1, 1, 0), ("s", -1, 0, 1, 1), ("s", 0, 1, 1, 1), ("s", 1, 0, 0, 0),
+    ("s", 1, 0, 0, 1), ("s", -1, 0, 0, 0), ("f", 0, 0, 0), ("f", 0, 0, 1), ("s", 0, 1, 0, 0), ("s", 1, 0, 1, 0),
+    ("c", 0, 0), ("s", -1, 0, 0, 1), ("s", 0, 1, 0, 1), ("s", 1, 0, 1, 1), ("s", -2, 0, 1, 0), ("s", -1, 1, 1, 0),
+    ("s", 2, 0, 0, 0), ("s", 1, 1, 0, 0), ("f", 0, 1, 1), ("s", -2, 0, 1, 1), ("f", -1, 0, 1), ("s", 2, 0, 0, 1),
+    ("f", 1, 0, 0), ("s", 1, 1, 0, 1), ("s", -1, 1, 1, 1), ("s", -2, 0, 0, 0), ("s", -1, 1, 0, 0),
+    ("s", 2, 0, 1, 0), ("f", 0, 1, 0), ("s", -2, 0, 0, 1), ("f", -1, 0, 0), ("s", -1, 1, 0, 1), ("s", 2, 0, 1, 1),
+    ("f", 1, 0, 1), ("s", 1, 1, 1, 0), ("s", -2, 1, 1, 0), ("s", -3, 0, 1, 0), ("s", 3, 0, 0, 0), ("s", 1, 1, 1, 1),
+    ("s", 2, 1, 0, 0), ("f", -2, 0, 1), ("s", -3, 0, 1, 1), ("f", 2, 0, 0), ("s", 3, 0, 0, 1), ("f", 1, 1, 0),
+    ("s", -2, 1, 0, 0), ("s", 2, 1, 0, 1), ("s", -3, 0, 0, 0), ("s", 3, 0, 1, 0), ("s", 2, 1, 1, 0),
+    ("f", -1, 1, 1), ("s", -2, 1, 1, 1), ("f", -2, 0, 0), ("s", -3, 0, 0, 1), ("d", 0, 0), ("s", -2, 1, 0, 1),
+    ("f", 2, 0, 1), ("s", 3, 0, 1, 1), ("c", 0, 1), ("c", -1, 0), ("s", 2, 1, 1, 1), ("f", -1, 1, 0),
+    ("s", 4, 0, 0, 0), ("s", 4, 0, 1, 0), ("s", -3, 1, 1, 0), ("f", -3, 0, 1), ("s", 4, 0, 1, 1), ("d", 0, 1),
+    ("s", 4, 0, 0, 1), ("s", -3, 1, 1, 1), ("f", 3, 0, 0), ("f", 1, 1, 1), ("s", 3, 1, 0, 0), ("s", -3, 1, 0, 0),
+    ("f", 2, 1, 0), ("d", -1, 0), ("f", -2, 1, 1), ("s", 3, 1, 0, 1), ("s", 3, 1, 1, 0), ("c", 1, 0), ("c", 1, 1),
+    ("f", -3, 0, 0), ("s", -3, 1, 0, 1), ("f", 3, 0, 1), ("f", -2, 1, 0), ("s", 4, 1, 1, 0), ("s", 3, 1, 1, 1),
+    ("s", 4, 1, 0, 0), ("f", 2, 1, 1), ("d", 1, 0), ("s", 4, 1, 1, 1), ("f", 4, 0, 0), ("f", 4, 0, 1), ("c", 2, 0),
+    ("c", -1, 1), ("c", 2, 1), ("c", -2, 0), ("s", 4, 1, 0, 1), ("d", 1, 1), ("f", -3, 1, 1), ("f", -3, 1, 0),
+    ("d", 2, 0), ("f", 3, 1, 0), ("d", -1, 1), ("f", 3, 1, 1), ("c", -3, 0), ("c", -2, 1), ("d", 2, 1), ("c", 3, 0),
+    ("c", 3, 1), ("d", -2, 0), ("f", 4, 1, 1), ("d", -3, 0), ("c", 4, 0), ("d", -2, 1), ("f", 4, 1, 0), ("d", 3, 0),
+    ("c", 4, 1), ("d", 3, 1), ("c", -3, 1), ("d", 4, 0), ("d", 4, 1), ("d", -3, 1),
 )
 
 SUM_ACROSS = (-2, -1, 0, 1, 2)
@@ -209,15 +217,19 @@
             s = op[3]
             for q in range(QG):
                 have(o, s, q)
-            start = mine + s * (HALF // 2)
-            for name, count in zip(("y_up", "y_down", "beyond"), SPLITS[SPLIT_AT[o[0] % NZ]][s]):
-                there = (o[0], 1 - o[1]) if name == "beyond" else o
-                if there != (0, 0):
+            base = mine + s * (HALF // 2)
+            there = (o[0], 1 - o[1])
+            near, far = SPLIT[*o, s], SPLIT[*there, s]
+            for name, place, start, count in (
+                ("y_up", o, 0, near[0]),
+                ("y_down", o, near[0], near[1]),
+                ("beyond", there, far[0] + far[1], far[2]),
+            ):
+                if count and place != (0, 0):
                     send(
-                        source(o, start, count), rows(o, start, count),
-                        send_sem.at[0], fin_sem.at[INDEX[there]], to[name],
+                        source(o, base + start, count), rows(o, base + start, count),
+                        send_sem.at[0], fin_sem.at[INDEX[place]], to[name],
                     )
-                start = start + count
         elif kind == "c":
             if o != (0, 0):
                 wait(rows(o, theirs, HALF), fin_sem.at[k])
@@ -272,8 +284,13 @@
     t_load.wait()
     for h in range(2):
         toks = slice(h * (TOK // 2), (h + 1) * (TOK // 2))
-        cot = (acc[toks, :] / root_width - tgt[toks, :].astype(F32)) * grad_scale
-        cot_own[h] = cot.T.astype(BF16)
+        cot = (acc[toks, :] * (1.0 / root_width) - tgt[toks, :].astype(F32)) * grad_scale
+        cot_t = cot.T.astype(BF16)
+        for j in range(NG):
+            for q in range(QR):
+                cot_own[h, q * PART + j * WIDTH : q * PART + (j + 1) * WIDTH, :] = cot_t[
+                    j * OWN + q * WIDTH : j * OWN + (q + 1) * WIDTH
+                ]
         send(cot_own.at[h], cot_par.at[h], send_sem.at[2], cot_sem.at[0], to["core"])
 
     w_t[...] = wfull[pl.ds(pl.multiple_of(f * ROWS, ROWS), ROWS), :].astype(F32).T
@@ -291,22 +308,18 @@
 
     def owner_part(s, q):
         part = pl.ds(q * PART, PART)
-        delta = (inner_rate * (total((0, 0), s, q) / root_width)).reshape(PART // BLOCK, BLOCK, LANES)
+        delta = (total((0, 0), s, q) * (inner_rate / root_width)).reshape(PART // BLOCK, BLOCK, LANES)
         largest = jnp.max(jnp.abs(delta), axis=1, keepdims=True)
         block_scale = jnp.exp2(jnp.ceil(jnp.log2(largest / 6.0 + 1e-30))).astype(BF16).astype(F32)
-        code = jnp.clip(delta / block_scale, -6.0, 6.0).astype(BF16)
+        code = jnp.clip(delta * (1.0 / block_scale), -6.0, 6.0).astype(BF16)
         dec[s, part, :] = (code.astype(F32) * block_scale).reshape(PART, LANES).astype(BF16)
-        for j in range(q * PART // OWN, (q + 1) * PART // OWN):
-            @pl.when(g != j)
-            def _(j=j):
-                send(
-                    dec.at[s, pl.ds(j * OWN, OWN)], gsum.at[s, g],
-                    send_sem.at[4], ex_sem.at[s], {"group": j, "fsdp": f},
-                )
-
-            @pl.when(g == j)
-            def _(j=j):
-                gsum[s, g] = dec[s, pl.ds(j * OWN, OWN), :]
+        for step in range(1, NG):
+            other = (g + step) % NG
+            send(
+                dec.at[s, pl.ds(pl.multiple_of(q * PART + other * WIDTH, WIDTH), WIDTH)],
+                gsum.at[s, g, pl.ds(q * WIDTH, WIDTH)], send_sem.at[4], ex_sem.at[s], {"group": other, "fsdp": f},
+            )
+        gsum[s, g, pl.ds(q * WIDTH, WIDTH), :] = dec[s, pl.ds(pl.multiple_of(q * PART + g * WIDTH, WIDTH), WIDTH), :]
 
     def sum_op(op):
         o, s, q = (op[1], op[2]), op[3], op[4]
@@ -361,7 +374,7 @@
         summed = gsum[s, 0].astype(F32)
         for step in range(1, NG):
             summed = summed + gsum[s, step].astype(F32)
-        average = summed / NG
+        average = summed * (1.0 / NG)
         lanes = slice(s * LANES, (s + 1) * LANES)
         new_mom = momentum_decay * mom[:, lanes] + average
         own_w = w_t[pl.ds(mine_rows, OWN), lanes]

time: 82.1 us -> 78.9 us (0.961)
  Pallas kernels: 80.9 us -> 77.9 us
    pallas_call x1, Pallas kernels: 79.1 us -> 76.2 us  [body(): pl.pallas_call(kernel, out_shape=(jax.ShapeDtypeStruct((KVW, ROWS), BF16)...]
where the time goes in v3:
time: 78.9 us; the launch traced here: 78.6 us
  Pallas kernels  77.9 us (99%)
    pallas_call x1, Pallas kernels, body(): pl.pallas_call(kernel, out_shape=(jax.ShapeDtypeStruct((KVW, ROWS), BF16)...  76.2 us
    pallas_call x1, Pallas kernels, body(): pl.pallas_call(finish, out_shape=(jax.ShapeDtypeStruct((ROWS, KVW), BF16)...  1.8 us

profile of v3, /device:TPU:2, one launch (start us, length us, event | category | flops | bytes accessed | tf_op | source)
XLA Modules:
  0.0 78.6 jit_solution(1517452374661130497)
XLA Ops:
  0.6 76.2 %shard_map.59 = (bf16[512,256]{1,0:T(8,128)(2,1)}, f32[64,256]{1,0:T(8,128)}) custom-call(bf16[512,8192]{1,0:T(8,128)(2,1)} %tok_hbm.1, bf16[512,512]{1,0:T(8,128)(2,1)} %tgt_hbm.1, bf16[256,512]{1,0:T(8,128)(2,1)} %w_hbm.1, f32[64,256]{1,0:T(8,128)} %bitcast.2), custom_call_target="tpu_custom_call" | custom-call | flops 8589934592 | bytes 8912896 | tf_op jit(solution)/shard_map/pallas_call | solution.py:413
  76.8 1.8 %shard_map.60 = (bf16[256,512]{1,0:T(8,128)(2,1)}, f32[64,256]{1,0:T(8,128)}) custom-call(bf16[512,256]{1,0:T(8,128)(2,1)} %get-tuple-element.6.nw_t, f32[64,256]{1,0:T(8,128)} %get-tuple-element.7.nm_t), custom_call_target="tpu_custom_call" | custom-call | tf_op jit(solution)/shard_map/pallas_call | solution.py:448

commit v4 on v3

--- a/solution.py
+++ b/solution.py
@@ -1,3 +1,4 @@
+import functools
 import math
 
 import jax
@@ -28,7 +29,16 @@
 PART = KVW // QR
 WIDTH = OWN // QR
 
-GATHER_ACROSS = (-2, -1, 0, 1, 3, 4)
+GATHER_TREE = {
+    (-3, 0, 0): ("down", (-2, 0)), (-3, 1, 0): ("down", (-2, 1)), (-2, 0, 0): ("down", (-1, 0)), (-2, 1, 0): ("across", (-2, 0)),
+    (-1, 0, 0): ("down", (0, 0)), (-1, 1, 0): ("across", (-1, 0)), (0, 1, 0): ("across", (0, 0)), (1, 0, 0): ("up", (0, 0)),
+    (1, 1, 0): ("across", (1, 0)), (2, 0, 0): ("up", (1, 0)), (2, 1, 0): ("up", (1, 1)), (3, 0, 0): ("up", (2, 0)),
+    (3, 1, 0): ("across", (3, 0)), (4, 0, 0): ("up", (3, 0)), (4, 1, 0): ("across", (4, 0)), (3, 0, 1): ("up", (2, 0)),
+    (3, 1, 1): ("up", (2, 1)), (2, 0, 1): ("up", (1, 0)), (2, 1, 1): ("across", (2, 0)), (1, 0, 1): ("up", (0, 0)),
+    (1, 1, 1): ("across", (1, 0)), (0, 1, 1): ("across", (0, 0)), (-1, 0, 1): ("down", (0, 0)), (-1, 1, 1): ("across", (-1, 0)),
+    (-2, 0, 1): ("down", (-1, 0)), (-2, 1, 1): ("down", (-1, 1)), (-3, 0, 1): ("down", (-2, 0)), (-3, 1, 1): ("across", (-3, 0)),
+    (4, 0, 1): ("down", (-3, 0)), (4, 1, 1): ("across", (4, 0)),
+}
 SPLIT = {
     (-3, 0, 0): (0, 64, 0), (-3, 0, 1): (16, 48, 0), (-3, 1, 0): (0, 64, 0), (-3, 1, 1): (64, 0, 0),
     (-2, 0, 0): (64, 0, 0), (-2, 0, 1): (48, 16, 0), (-2, 1, 0): (0, 0, 64), (-2, 1, 1): (64, 0, 0),
@@ -64,21 +74,21 @@
 
 SUM_ACROSS = (-2, -1, 0, 1, 2)
 SUM = (
-    ("u", 1, 1), ("p", 1, 1, 0, 0), ("p", 1, 1, 0, 1), ("u", 4, 1), ("p", 4, 1, 0, 0), ("p", 4, 1, 1, 0),
-    ("p", 4, 1, 0, 1), ("p", 4, 1, 1, 1), ("u", 2, 0), ("u", -1, 0), ("p", 1, 1, 1, 0), ("u", 3, 1),
-    ("p", 3, 1, 1, 0), ("u", -3, 1), ("p", -3, 1, 0, 0), ("u", -2, 1), ("p", 1, 1, 1, 1), ("u", 4, 0),
-    ("p", 4, 0, 0, 0), ("p", 4, 0, 1, 0), ("u", -1, 1), ("u", 1, 0), ("p", -1, 1, 0, 0), ("u", -3, 0),
-    ("p", 3, 1, 0, 0), ("p", -3, 1, 1, 0), ("u", 0, 0), ("p", -1, 1, 1, 0), ("u", 2, 1), ("u", 0, 1),
-    ("p", 3, 1, 0, 1), ("p", -3, 1, 1, 1), ("u", 3, 0), ("p", 2, 1, 1, 0), ("u", -2, 0), ("p", 4, 0, 0, 1),
-    ("p", 4, 0, 1, 1), ("p", -2, 1, 0, 0), ("p", 3, 1, 1, 1), ("p", -3, 0, 1, 0), ("p", -2, 1, 1, 0),
-    ("p", 3, 0, 1, 0), ("p", -3, 0, 0, 0), ("p", -2, 1, 1, 1), ("p", 3, 0, 1, 1), ("p", -3, 1, 0, 1),
-    ("p", 2, 1, 0, 0), ("p", 3, 0, 0, 0), ("p", -3, 0, 1, 1), ("p", 2, 1, 1, 1), ("p", 3, 0, 0, 1),
-    ("p", -3, 0, 0, 1), ("p", 2, 1, 0, 1), ("p", 2, 0, 1, 0), ("p", -2, 0, 1, 0), ("p", -2, 1, 0, 1),
-    ("p", -2, 0, 0, 0), ("p", 2, 0, 0, 0), ("p", -1, 1, 0, 1), ("p", -2, 0, 1, 1), ("p", 2, 0, 1, 1),
-    ("p", -1, 1, 1, 1), ("p", 2, 0, 0, 1), ("p", -1, 0, 1, 0), ("p", 0, 1, 1, 0), ("p", 1, 0, 1, 0),
-    ("p", -2, 0, 0, 1), ("p", 0, 1, 0, 0), ("p", 1, 0, 0, 0), ("p", -1, 0, 0, 0), ("p", 0, 1, 1, 1),
-    ("p", 1, 0, 1, 1), ("p", -1, 0, 1, 1), ("p", 0, 1, 0, 1), ("p", 1, 0, 0, 1), ("p", 0, 0, 1, 0),
-    ("p", -1, 0, 0, 1), ("p", 0, 0, 0, 0), ("p", 0, 0, 1, 1), ("p", 0, 0, 0, 1),
+    ("u", 4, 1), ("p", 4, 1, 1, 0), ("p", 4, 1, 1, 1), ("p", 4, 1, 0, 0), ("p", 4, 1, 0, 1), ("u", 1, 1),
+    ("p", 1, 1, 1, 0), ("p", 1, 1, 1, 1), ("u", -2, 1), ("u", -3, 1), ("p", -3, 1, 0, 0), ("u", 3, 0),
+    ("p", 1, 1, 0, 0), ("p", 3, 0, 1, 0), ("u", -2, 0), ("u", 3, 1), ("p", 3, 1, 1, 0), ("p", -3, 1, 0, 1),
+    ("u", 0, 0), ("p", 1, 1, 0, 1), ("u", -1, 1), ("u", -1, 0), ("p", 3, 1, 0, 0), ("p", -3, 1, 1, 0), ("u", 1, 0),
+    ("p", -1, 1, 0, 0), ("u", 2, 0), ("p", -3, 1, 1, 1), ("p", 3, 1, 0, 1), ("u", 4, 0), ("p", -1, 1, 0, 1),
+    ("u", 0, 1), ("u", -3, 0), ("p", 4, 0, 1, 0), ("p", 3, 1, 1, 1), ("u", 2, 1), ("p", -2, 1, 0, 0),
+    ("p", 4, 0, 1, 1), ("p", 4, 0, 0, 0), ("p", 2, 1, 1, 0), ("p", -3, 0, 0, 0), ("p", 4, 0, 0, 1),
+    ("p", -2, 1, 1, 0), ("p", -3, 0, 0, 1), ("p", 3, 0, 1, 1), ("p", 2, 1, 0, 0), ("p", -3, 0, 1, 0),
+    ("p", 2, 1, 1, 1), ("p", 3, 0, 0, 0), ("p", -3, 0, 1, 1), ("p", 2, 0, 1, 0), ("p", -2, 1, 1, 1),
+    ("p", -2, 0, 0, 0), ("p", 3, 0, 0, 1), ("p", 2, 1, 0, 1), ("p", -2, 1, 0, 1), ("p", -2, 0, 1, 0),
+    ("p", 2, 0, 0, 0), ("p", 2, 0, 1, 1), ("p", -1, 1, 1, 0), ("p", -2, 0, 1, 1), ("p", 1, 0, 1, 0),
+    ("p", -1, 1, 1, 1), ("p", -1, 0, 0, 0), ("p", 2, 0, 0, 1), ("p", 0, 1, 1, 0), ("p", -2, 0, 0, 1),
+    ("p", 1, 0, 0, 0), ("p", 0, 1, 0, 0), ("p", -1, 0, 1, 0), ("p", 1, 0, 1, 1), ("p", 0, 1, 1, 1),
+    ("p", -1, 0, 1, 1), ("p", 0, 1, 0, 1), ("p", 1, 0, 0, 1), ("p", -1, 0, 0, 1), ("p", 0, 0, 1, 0),
+    ("p", 0, 0, 0, 0), ("p", 0, 0, 1, 1), ("p", 0, 0, 0, 1),
 )
 
 OFFSETS = tuple((oz, ox) for ox in range(2) for oz in (0, 1, -1, 2, -2, 3, -3, 4))
@@ -107,7 +117,6 @@
     return parent
 
 
-GATHER_TREE = tree(GATHER_ACROSS)
 SUM_TREE = tree(SUM_ACROSS)
 
 
@@ -116,10 +125,33 @@
 
 
 def pick(k, table):
-    got = jnp.int32(table[0])
-    for at in range(1, len(table)):
-        got = jnp.where(k == at, jnp.int32(table[at]), got)
-    return got
+    if len(table) == 1:
+        return jnp.int32(table[0])
+    half = 1 << (len(table) - 1).bit_length() - 1
+    return jnp.where(k < half, pick(k, table[:half]), pick(k - half, table[half:]))
+
+
+def dispatch(t, acts, width=4):
+    for low in range(0, len(acts), width):
+        block = [(n, acts[n]) for n in range(low, min(low + width, len(acts))) if acts[n]]
+        if block:
+            @pl.when((t >= low) & (t < low + width))
+            def _(block=block):
+                for n, act in block:
+                    pl.when(t == n)(act)
+
+
+def all_of(act, ops):
+    for op in ops:
+        act(op)
+
+
+def quo(a, b):
+    return lax.div(a, jnp.int32(b))
+
+
+def rem(a, b):
+    return lax.rem(a, jnp.int32(b))
 
 
 def encoded(offsets):
@@ -134,19 +166,19 @@
 ):
     g = lax.axis_index("group")
     f = lax.axis_index("fsdp")
-    xh, y = g // NY, g % NY
-    z, xl, c = f // (NX * NC), (f // NC) % NX, f % NC
+    xh, y = quo(g, NY), rem(g, NY)
+    z, xl, c = quo(f, NX * NC), rem(quo(f, NC), NX), rem(f, NC)
 
     def at(zz, xx, cc):
         return (zz * NX + xx) * NC + cc
 
     to = {
-        "up": {"group": g, "fsdp": at((z + 1) % NZ, xl, c)},
-        "down": {"group": g, "fsdp": at((z + NZ - 1) % NZ, xl, c)},
+        "up": {"group": g, "fsdp": at(rem(z + 1, NZ), xl, c)},
+        "down": {"group": g, "fsdp": at(rem(z + NZ - 1, NZ), xl, c)},
         "across": {"group": g, "fsdp": at(z, 1 - xl, c)},
         "core": {"group": g, "fsdp": at(z, xl, 1 - c)},
-        "y_up": {"group": xh * NY + (y + 1) % NY, "fsdp": f},
-        "y_down": {"group": xh * NY + (y + NY - 1) % NY, "fsdp": f},
+        "y_up": {"group": xh * NY + rem(y + 1, NY), "fsdp": f},
+        "y_down": {"group": xh * NY + rem(y + NY - 1, NY), "fsdp": f},
         "beyond": {"group": (1 - xh) * NY + y, "fsdp": at(z, 1 - xl, c)},
     }
 
@@ -163,7 +195,8 @@
         pltpu.make_async_copy(ref, ref, sem).wait()
 
     def chip_of(enc):
-        return (z + NZ - enc // 2) % NZ, (xl + enc) % 2
+        enc = jnp.int32(enc)
+        return rem(z + NZ - quo(enc, 2), NZ), rem(xl + enc, 2)
 
     def shard_of(o):
         zz, xx = chip_of((o[0] % NZ) * 2 + o[1])
@@ -185,11 +218,12 @@
 
     pl.semaphore_wait(barrier, len(to))
 
-    mine = pl.multiple_of(((y + xh) % 2) * HALF, HALF)
+    row_of = {o: shard_of(o) * ROWS for o in OFFSETS}
+    mine = pl.multiple_of(rem(y + xh, 2) * HALF, HALF)
     theirs = pl.multiple_of(HALF - mine, HALF)
 
     def rows(o, start, count):
-        return wfull.at[pl.ds(pl.multiple_of(shard_of(o) * ROWS + start, 16), count)]
+        return wfull.at[pl.ds(pl.multiple_of(row_of[o] + start, 16), count)]
 
     def source(o, start, count):
         return w_hbm.at[pl.ds(pl.multiple_of(start, 16), count)] if o == (0, 0) else rows(o, start, count)
@@ -206,7 +240,7 @@
         k = INDEX[o]
         if kind == "s":
             s, q = op[3:]
-            direction, before = GATHER_TREE[o, s]
+            direction, before = GATHER_TREE[*o, s]
             have(before, s, q)
             start = mine + (s * QG + q) * PIECE
             send(
@@ -257,20 +291,16 @@
 
     @pl.loop(0, N)
     def _(t):
-        for n in range(N):
-            if groups[n]:
-                @pl.when(t == n)
-                def _(n=n):
-                    for op in groups[n]:
-                        gather_op(op)
+        dispatch(t, [functools.partial(all_of, gather_op, ops) if ops else None for ops in groups[:N]])
 
         @pl.when(t == 0)
         def _():
             w_load.wait()
             wait(x_own, load_sem.at[1])
 
-        zz, xx = chip_of(pick(t, encoded(order)))
-        k = pick(t, [INDEX[o] for o in order])
+        step = pick(t, [INDEX[o] * 16 + e for o, e in zip(order, encoded(order))])
+        k = quo(step, 16)
+        zz, xx = chip_of(rem(step, 16))
         a, b = at(zz, xx, c), at(zz, xx, 1 - c)
         rows_a = pl.ds(pl.multiple_of(a * ROWS, ROWS), ROWS)
         rows_b = pl.ds(pl.multiple_of(b * ROWS, ROWS), ROWS)
@@ -314,7 +344,7 @@
         code = jnp.clip(delta * (1.0 / block_scale), -6.0, 6.0).astype(BF16)
         dec[s, part, :] = (code.astype(F32) * block_scale).reshape(PART, LANES).astype(BF16)
         for step in range(1, NG):
-            other = (g + step) % NG
+            other = rem(g + step, NG)
             send(
                 dec.at[s, pl.ds(pl.multiple_of(q * PART + other * WIDTH, WIDTH), WIDTH)],
                 gsum.at[s, g, pl.ds(q * WIDTH, WIDTH)], send_sem.at[4], ex_sem.at[s], {"group": other, "fsdp": f},
@@ -344,8 +374,9 @@
 
     @pl.loop(0, N)
     def _(t):
-        zz, xx = chip_of(pick(t, encoded(sum_order)))
-        k = pick(t, [INDEX[o] for o in sum_order])
+        step = pick(t, [INDEX[o] * 16 + e for o, e in zip(sum_order, encoded(sum_order))])
+        k = quo(step, 16)
+        zz, xx = chip_of(rem(step, 16))
         x_a, x_b = x_own[at(zz, xx, c)], x_oth[zz * NX + xx]
         half = TOK // 2
         grad = jnp.dot(cot_own[0], x_a[:half], preferred_element_type=F32)
@@ -355,12 +386,7 @@
         for s in range(2):
             gbuf[k, s] = grad[:, s * LANES : (s + 1) * LANES]
             sbuf[k, s] = grad[:, s * LANES : (s + 1) * LANES].astype(BF16)
-        for n in range(N - 1):
-            if sum_groups[n + 1]:
-                @pl.when(t == n)
-                def _(n=n):
-                    for op in sum_groups[n + 1]:
-                        sum_op(op)
+        dispatch(t, [functools.partial(all_of, sum_op, ops) if ops else None for ops in sum_groups[1:N]])
 
     for op in sum_groups[N]:
         sum_op(op)
@@ -382,7 +408,7 @@
         for step in range(1, NG):
             send(
                 upd.at[s], nw_hbm.at[pl.ds(mine_rows, OWN), pl.ds(s * LANES, LANES)], send_sem.at[5], up_sem.at[0],
-                {"group": (g + step) % NG, "fsdp": f},
+                {"group": rem(g + step, NG), "fsdp": f},
             )
         pltpu.make_async_copy(
             upd.at[s], nw_hbm.at[pl.ds(mine_rows, OWN), pl.ds(s * LANES, LANES)], out_sem.at[1]

time: 78.9 us -> 78.2 us (level)
  no operation moved by 1% of the time
where the time goes in v4:
time: 78.2 us; the launch traced here: 77.9 us
  Pallas kernels  77.3 us (99%)
    pallas_call x1, Pallas kernels, body(): pl.pallas_call(kernel, out_shape=(jax.ShapeDtypeStruct((KVW, ROWS), BF16)...  75.5 us
    pallas_call x1, Pallas kernels, body(): pl.pallas_call(finish, out_shape=(jax.ShapeDtypeStruct((ROWS, KVW), BF16)...  1.8 us

profile of v4, /device:TPU:2, one launch (start us, length us, event | category | flops | bytes accessed | tf_op | source)
XLA Modules:
  0.0 77.9 jit_solution(12863151069394554840)
XLA Ops:
  0.6 75.5 %shard_map.59 = (bf16[512,256]{1,0:T(8,128)(2,1)}, f32[64,256]{1,0:T(8,128)}) custom-call(bf16[512,8192]{1,0:T(8,128)(2,1)} %tok_hbm.1, bf16[512,512]{1,0:T(8,128)(2,1)} %tgt_hbm.1, bf16[256,512]{1,0:T(8,128)(2,1)} %w_hbm.1, f32[64,256]{1,0:T(8,128)} %bitcast.2), custom_call_target="tpu_custom_call" | custom-call | flops 8589934592 | bytes 8912896 | tf_op jit(solution)/shard_map/pallas_call | solution.py:439
  76.1 1.8 %shard_map.60 = (bf16[256,512]{1,0:T(8,128)(2,1)}, f32[64,256]{1,0:T(8,128)}) custom-call(bf16[512,256]{1,0:T(8,128)(2,1)} %get-tuple-element.6.nw_t, f32[64,256]{1,0:T(8,128)} %get-tuple-element.7.nm_t), custom_call_target="tpu_custom_call" | custom-call | tf_op jit(solution)/shard_map/pallas_call | solution.py:474
